TPU v7x, 32 devices: a whole 2x2x4 slice. The times are simulated.
32 devices in a mesh: parts: 2 (over y), track: 4 (over z), tm: 2 (over x), coef: 2 (over core).
Axes of the slice: x: 2, y: 2, z: 4, core: 2. Of those that a mesh axis runs over, the one named last changes fastest.
Arguments:
- sector_ids: int32 [12288], P(('parts', 'track', 'tm')), parts along dimension 0, may hold values from 0 to 63, as said below
- observed: float32 [3, 12288], P(None, ('parts', 'track', 'tm')), parts along dimension 1, may hold values from -6 to 6
- weights: float32 [3, 12288], P(None, ('parts', 'track', 'tm')), parts along dimension 1, may hold values from 0.3 to 3
- coefficients: float32 [2048, 128], P(('parts', 'track')), parts along dimension 0, may hold values from -6 to 6
- tile_index: int32 [128, 12], P(('parts', 'track', 'tm'), 'coef'), parts along dimension 0, may hold values from 0 to 1023, as said below
- tile_count: int32 [128], P(('parts', 'track', 'tm')), parts along dimension 0, may hold values from 3 to 12
- sensitivity: bfloat16 [128, 12, 3, 128, 128], P(('parts', 'track', 'tm'), 'coef'), parts along dimension 0, may hold values from -0.15625 to 0.15625
Outputs:
- gradient: float32 [2048, 128], P(('parts', 'track')), parts along dimension 0
There are 2 independent parts, one for each index of `parts`. A program takes and returns all parts, laid end to end along the dimension named above; each array names one. Nothing has to cross between parts.
Inputs may be any that keep to these rules, and one draw needn't show every extreme that they name: `sector_ids`: the rows of one index of track and tm fall in at most 192 rows into the 8 consecutive sectors of any one index, and some pair reaches 192; the sectors of each index receive exactly 768 rows in all; each sector holds at most 128 rows, and every index holds a sector with exactly 128. `tile_index`: entries at positions from tile_count on are arbitrary blocks and take no part. Block n belongs to track index n // 256. Of the 48 entries held by one index of track, tm and coef (its sectors' rows, its coef share of the columns), live or not, at most 24 name blocks of any one track index, and every such device has a track index named exactly 24 times.
All inputs are finite; a program needn't handle non-finite values.
Results may differ from a plain program's by a relative error of at most 0.0037.
Values may be sent and summed in bfloat16 or wider, within the bound.
A program may use at most 64 MiB of HBM per device.

v0:
```python
import jax
import jax.numpy as jnp
from jax import lax
from jax.sharding import PartitionSpec as P

HUBER = 2.0


def per_device(sector_ids, observed, weights, coefficients, tile_index, tile_count, sensitivity):
    sector_total = tile_index.shape[0]
    half_k = tile_index.shape[1]
    slot_count = sensitivity.shape[3]
    block_width = sensitivity.shape[4]
    owners = lax.axis_size(("track", "tm"))
    row_total = sector_ids.shape[0]
    capacity = 2 * row_total // owners
    rounded = coefficients.astype(jnp.bfloat16)
    every_block = lax.all_gather(rounded, "track", axis=0, tiled=True)
    owner_of = sector_ids // sector_total
    local_sector = sector_ids % sector_total
    onehot = (owner_of[:, None] == jnp.arange(owners, dtype=jnp.int32)[None, :]).astype(jnp.int32)
    ranking = jnp.sum((jnp.cumsum(onehot, axis=0) - 1) * onehot, axis=1)
    placing = owner_of * capacity + ranking
    payload = jnp.concatenate([observed, weights], axis=0)
    outgoing = jnp.zeros((6, owners * capacity), jnp.float32).at[:, placing].set(payload)
    outgoing = jnp.transpose(outgoing.reshape(6, owners, capacity), (1, 0, 2))
    labels = jnp.full((owners * capacity,), -1, jnp.int32).at[placing].set(local_sector)
    labels = labels.reshape(owners, capacity)
    got_rows, got_labels = (
        lax.all_to_all(outgoing, ("track", "tm"), split_axis=0, concat_axis=0, tiled=True),
        lax.all_to_all(labels, ("track", "tm"), split_axis=0, concat_axis=0, tiled=True),
    )
    received = jnp.transpose(got_rows, (1, 0, 2)).reshape(6, owners * capacity)
    flat_labels = got_labels.reshape(owners * capacity)
    member = (flat_labels[:, None] == jnp.arange(sector_total, dtype=jnp.int32)[None, :]).astype(
        jnp.int32
    )
    within = jnp.sum((jnp.cumsum(member, axis=0) - 1) * member, axis=1)
    target = jnp.where(
        flat_labels >= 0, flat_labels * slot_count + within, sector_total * slot_count
    )
    gridded = jnp.zeros((6, sector_total * slot_count + 1), jnp.float32).at[:, target].set(received)
    gridded = jnp.transpose(gridded[:, :-1].reshape(6, sector_total, slot_count), (1, 0, 2))
    observed_tiles = gridded[:, :3]
    weight_tiles = gridded[:, 3:]
    k_global = lax.axis_index("coef") * half_k + jnp.arange(half_k, dtype=jnp.int32)
    active = k_global[None, :] < tile_count[:, None]
    blocks = jnp.take(every_block, tile_index, axis=0)
    blocks = jnp.where(active[:, :, None], blocks, jnp.zeros_like(blocks))
    partial_pred = jnp.einsum(
        "skcjb,skb->scj", sensitivity, blocks, preferred_element_type=jnp.float32
    )
    predicted = lax.psum(partial_pred, "coef")
    scaled = weight_tiles * (predicted - observed_tiles)
    force = (weight_tiles * scaled / jnp.sqrt(1.0 + (scaled / HUBER) ** 2)).astype(jnp.bfloat16)
    tile_grad = jnp.einsum("skcjb,scj->skb", sensitivity, force, preferred_element_type=jnp.float32)
    tile_grad = jnp.where(active[:, :, None], tile_grad, jnp.zeros_like(tile_grad))
    block_total = every_block.shape[0]
    partial_grad = jnp.zeros((block_total, block_width), jnp.float32)
    partial_grad = partial_grad.at[tile_index.reshape(-1)].add(tile_grad.reshape(-1, block_width))
    summed = lax.psum_scatter(partial_grad, "track", scatter_dimension=0, tiled=True)
    gradient = lax.psum(summed, ("tm", "coef"))
    return gradient


def solution(mesh):
    placed = (
        P(("parts", "track", "tm")),
        P(None, ("parts", "track", "tm")),
        P(None, ("parts", "track", "tm")),
        P(("parts", "track"), None),
        P(("parts", "track", "tm"), "coef"),
        P(("parts", "track", "tm")),
        P(("parts", "track", "tm"), "coef", None, None, None),
    )
    return jax.shard_map(
        per_device,
        mesh=mesh,
        in_specs=placed,
        out_specs=P(("parts", "track"), None),
        check_vma=False,
    )
```

profile of v0, /device:TPU:0, one launch (start us, length us, event | category | flops | bytes accessed | tf_op | source)
XLA Modules:
  0.0 135.0 jit_solution(9949122944024813271)
XLA Ops:
  6.5 0.7 add_select_fusion
  7.2 1.7 %reduce-window.14 = s32[8,6,128]{2,0,1:T(8,128)S(1)} reduce-window(s32[8,6,128]{2,0,1:T(8,128)S(1)} %fusion.13, s32[]{:T(128)} %constant.40.clone.1), window={size=1x1x128 pad=0_0x0_0x127_0}, to_apply=%region_0.1 | reduce-window | flops 780288 | bytes 49156 | tf_op jit(solution)/shard_map/reduce-window
  8.9 0.1 slice.30
  9.0 0.1 copy.24
  9.2 0.2 reduce-window.15
  9.3 0.1 copy.25
  9.4 0.1 fusion.11
  9.5 3.4 %scatter_custom_fusion = s32[1536]{0:T(1024)S(1)} fusion(s32[768]{0:T(1024)S(1)} %compare_select_fusion.2, s32[768]{0:T(1024)S(1)} %get-tuple-element.7, s32[]{:T(128)} %constant.74.clone.1), kind=kCustom, calls=%fused_computation.50 | custom fusion | bytes 6148 | tf_op jit(solution)/shard_map/scatter | solution.py:27
  12.9 0.7 all_to_all.9
  13.6 7.3 %all-to-all-start = ((s32[8,1,192]{2,1,0:T(1,128)}), s32[8,1,192]{2,1,0:T(1,128)S(1)}, u32[]{:S(2)}, u32[]{:S(2)}) async-start(s32[8,1,192]{2,1,0:T(1,128)} %all_to_all.9), calls=%async_computation | async-start | bytes 16384 | tf_op jit(solution)/shard_map/all_to_all | solution.py:31
  20.8 0.7 compare_select_fusion.1
  21.5 0.8 reshape.166
  22.3 0.7 maximum_bitcast_fusion
  23.0 0.2 copy.26
  23.2 4.4 %scatter_custom_fusion.1 = f32[6,1536]{0,1:T(8,128)S(1)} fusion(s32[768]{0:T(1024)S(1)} %compare_select_fusion.2, f32[768,6]{1,0:T(8,128)S(1)} %copy.26, f32[]{:T(128)} %constant.39.clone.1), kind=kCustom, calls=%fused_computation.7 | custom fusion | bytes 36868 | tf_op jit(solution)/shard_map/scatter | solution.py:25
  27.6 1.0 copy.27
  28.6 0.9 convert_element_type.18
  29.5 14.5 %all_gather.3 = bf16[1024,128]{1,0:T(8,128)(2,1)S(1)} all-gather(bf16[256,128]{1,0:T(8,128)(2,1)S(1)} %convert_element_type.18), channel_id=1, replica_groups=mesh['parts'=2,'track'=4,'tm'=2,'coef'=2] {'track'}, dimensions={0}, use_global_device_ids=true | all-gather | bytes 327680 | tf_op jit(solution)/shard_map/all_gather | solution.py:18
  44.0 0.1 reshape.175
  44.0 0.6 gather_fusion
  44.7 0.8 compare_and_fusion
  45.4 0.1 select_bitcast_fusion
  45.5 3.7 %fusion = f32[8,1,3,128,1]{3,1,4,2,0:T(1,128)S(1)} fusion(bf16[8,6,3,128,128]{4,3,2,1,0:T(8,128)(2,1)} %param.13, bf16[8,6,128,1,1]{2,1,0,3,4:T(8,128)(2,1)S(1)} %select_bitcast_fusion), kind=kOutput, calls=%fused_computation.5 | convolution fusion | flops 4718592 | bytes 4743168 | tf_op jit(solution)/shard_map/skcjb,skb->scj/dot_general | solution.py:50
  49.2 3.3 %psum.14 = f32[8,3,128]{2,0,1:T(8,128)S(1)} all-reduce(f32[8,3,128]{2,0,1:T(8,128)S(1)} %bitcast.50), channel_id=1, replica_groups=mesh['parts'=2,'track'=4,'tm'=2,'coef'=2] {'coef'}, use_global_device_ids=true, to_apply=%region_9.10 | all-reduce | flops 3072 | bytes 24576 | tf_op jit(solution)/shard_map/psum | solution.py:53
  52.5 5.7 %all-to-all-start.1 = ((f32[8,6,192]{2,1,0:T(8,128)}), f32[8,6,192]{2,1,0:T(8,128)S(1)}, u32[]{:S(2)}, u32[]{:S(2)}) async-start(f32[8,6,192]{2,1,0:T(8,128)} %bitcast.8), calls=%async_computation.1 | async-start | bytes 131072 | tf_op jit(solution)/shard_map/all_to_all | solution.py:30
  58.2 0.0 reduce-scatter.2.cloned.1.call-start
  58.3 0.1 eq.61
  58.4 0.1 eq.57
  58.5 2.3 %reduce-window.16 = s32[8,12,128]{2,1,0:T(8,128)S(1)} reduce-window(s32[8,12,128]{2,1,0:T(8,128)S(1)} %fusion.8, s32[]{:T(128)} %constant.40.clone.1), window={size=1x1x128 pad=0_0x0_0x127_0}, to_apply=%region_4.5 | reduce-window | flops 1560576 | bytes 98308 | tf_op jit(solution)/shard_map/reduce-window.2
  60.7 0.3 slice_reduce_fusion
  61.0 0.2 reduce-window.19
  61.2 0.1 add_bitcast_fusion
  61.3 0.1 mul.43
  61.4 0.1 ge.21
  61.6 3.5 %all-to-all-done.1 = f32[8,6,192]{2,1,0:T(8,128)S(1)} async-done(((f32[8,6,192]{2,1,0:T(8,128)}), f32[8,6,192]{2,1,0:T(8,128)S(1)}, u32[]{:S(2)}, u32[]{:S(2)}) %all-to-all-start.1) | async-done | bytes 36896 | tf_op jit(solution)/shard_map/all_to_all | solution.py:30
  65.1 0.1 reshape.198
  65.2 0.3 copy.29
  65.5 4.4 %scatter_custom_fusion.2 = f32[6,1025]{0,1:T(8,128)S(1)} fusion(s32[1536]{0:T(1024)S(1)} %fusion.17, f32[1536,6]{1,0:T(8,128)S(1)} %copy.29, f32[]{:T(128)} %constant.39.clone.1), kind=kCustom, calls=%fused_computation.9 | custom fusion | bytes 24604 | tf_op jit(solution)/shard_map/scatter | solution.py:42
  70.0 0.2 copy.36
  70.2 3.1 %fusion.15 = f32[8,1,6,128,1]{3,1,4,2,0:T(1,128)S(1)} fusion(bf16[8,6,3,128,128]{4,3,2,1,0:T(8,128)(2,1)} %param.13, bf16[8,3,128,1,1]{2,0,1,3,4:T(8,128)(2,1)S(1)} %fusion.18), kind=kOutput, calls=%fused_computation.34 | convolution fusion | flops 4718592 | bytes 4749312 | tf_op jit(solution)/shard_map/skcjb,scj->skb/dot_general | solution.py:56
  73.3 0.1 bitcast_select_fusion
  73.4 1.5 %scatter_custom_fusion.3 = f32[1024,128]{1,0:T(8,128)} fusion(s32[48]{0:T(128)S(1)} %fusion.23, f32[48,128]{1,0:T(8,128)S(1)} %reshape.209, f32[]{:T(128)} %constant.39.clone.1), kind=kCustom, calls=%fused_computation.11 | custom fusion | flops 6144 | bytes 524292 | tf_op jit(solution)/shard_map/scatter-add | solution.py:60
  74.9 0.0 reduce-scatter.2.cloned.1.call-update
  75.0 0.0 all-reduce.2.cloned.1.call-start
  75.0 19.6 %reduce-scatter.2.cloned.1.call-done = f32[256,128]{1,0:T(8,128)} async-done(((f32[1024,128]{1,0:T(8,128)}), f32[256,128]{1,0:T(8,128)}) %reduce-scatter.2.cloned.1.call-update) | async-done | bytes 131088 | tf_op jit(solution)/shard_map/reduce_scatter | solution.py:61
  94.6 0.0 all-reduce.2.cloned.1.call-update
  94.7 32.0 %all-reduce.2.cloned.1.call-done = f32[256,128]{1,0:T(8,128)} async-done(((f32[256,128]{1,0:T(8,128)}), f32[256,128]{1,0:T(8,128)}) %all-reduce.2.cloned.1.call-update) | async-done | bytes 131088 | tf_op jit(solution)/shard_map/psum | solution.py:62
  126.6 1.6 %copy.49 = f32[256,128]{1,0:T(8,128)} copy(f32[256,128]{1,0:T(8,128)} %all-reduce.2.cloned.1.call-done) | data formatting | bytes 262144
  (17 shorter events, 0.3 us)
Async XLA Ops:
  13.6 38.9 %all-to-all-start = ((s32[8,1,192]{2,1,0:T(1,128)}), s32[8,1,192]{2,1,0:T(1,128)S(1)}, u32[]{:S(2)}, u32[]{:S(2)}) async-start(s32[8,1,192]{2,1,0:T(1,128)} %all_to_all.9), calls=%async_computation | async-start | bytes 16384 | tf_op jit(solution)/shard_map/all_to_all | solution.py:31
  52.5 12.6 %all-to-all-start.1 = ((f32[8,6,192]{2,1,0:T(8,128)}), f32[8,6,192]{2,1,0:T(8,128)S(1)}, u32[]{:S(2)}, u32[]{:S(2)}) async-start(f32[8,6,192]{2,1,0:T(8,128)} %bitcast.8), calls=%async_computation.1 | async-start | bytes 131072 | tf_op jit(solution)/shard_map/all_to_all | solution.py:30
  58.2 36.4 %reduce-scatter.2.cloned.1.call-start = ((), (), s32[]{:S(2)}) async-start(), calls=%async_computation.3 | async-start | bytes 655360 | tf_op jit(solution)/shard_map/reduce_scatter | solution.py:61
  75.0 51.7 %all-reduce.2.cloned.1.call-start = ((), (), s32[]{:S(2)}) async-start(), calls=%async_computation.4 | async-start | bytes 262144 | tf_op jit(solution)/shard_map/psum | solution.py:62
Sparse Core Ops, SparseCore 0:
  75.1 19.5 reduce-scatter.1
  97.0 29.6 all-reduce.1
where the time goes:
time: 136 us; the launch traced here: 135 us
  waiting for transfers between devices  55.2 us (41%)
  local copies, waits for them, and re-layouts  18.6 us (14%)
  blocking collectives  17.8 us (13%)
  between operations  13.5 us (10%)
  starting transfers between devices  13.1 us (10%)
  other arithmetic  10.2 us (7%)
  matrix products  6.73 us (5%)
    psum x1, waiting for transfers between devices, per_device(): gradient = lax.psum(summed, ('tm', 'coef'))  32 us
    reduce_scatter x1, waiting for transfers between devices, per_device(): lax.psum_scatter(partial_grad, 'track', scatter_dimension=0, tiled=True)  19.6 us
    all_gather x1, blocking collectives, per_device(): every_block = lax.all_gather(rounded, 'track', axis=0, tiled=True)  14.5 us
    all_to_all x1, starting transfers between devices, per_device(): lax.all_to_all(labels, ('track', 'tm'), split_axis=0, concat_axis=0, tile...  7.25 us
    all_to_all x1, starting transfers between devices, per_device(): lax.all_to_all(outgoing, ('track', 'tm'), split_axis=0, concat_axis=0, ti...  5.72 us
    scatter x1, local copies, waits for them, and re-layouts, per_device(): jnp.zeros((6, sector_total * slot_count + 1), jnp.float32).at[:, target]  4.45 us
    scatter x1, local copies, waits for them, and re-layouts, per_device(): jnp.zeros((6, owners * capacity), jnp.float32).at[:, placing].set(payload)  4.36 us
    another operation x4, other arithmetic  4.31 us
  transfers between devices with their start and end apart: 4, of which 3 were waited for; matrix products, arithmetic and copies ran while one was open for 13% of the time, Pallas kernels for 0%

commit v1 on v0

--- a/solution.py
+++ b/solution.py
@@ -59,7 +59,11 @@
     partial_grad = jnp.zeros((block_total, block_width), jnp.float32)
     partial_grad = partial_grad.at[tile_index.reshape(-1)].add(tile_grad.reshape(-1, block_width))
     summed = lax.psum_scatter(partial_grad, "track", scatter_dimension=0, tiled=True)
-    gradient = lax.psum(summed, ("tm", "coef"))
+
+    def try_all_quarters(array_in, row_axis, mesh_ax):
+        return lax.psum(lax.psum(array_in, row_axis), mesh_ax)
+
+    gradient = try_all_quarters(summed, "coef", "tm")
     return gradient
 
 

time: 136 us -> 147 us (1.081)
  waiting for transfers between devices: 55.2 us -> 66.5 us
    psum x1 -> x2, waiting for transfers between devices: 32 us -> 43.3 us  [try_all_quarters(): return lax.psum(lax.psum(array_in, row_axis), mesh_ax)]
  transfers between devices with their start and end apart: 4 -> 5, of which waited for: 3 -> 4; matrix products, arithmetic and copies ran while one was open for 13% -> 12% of each run, Pallas kernels for 0% -> 0%
where the time goes in v1:
time: 147 us; the launch traced here: 146 us
  waiting for transfers between devices  66.5 us (45%)
  local copies, waits for them, and re-layouts  18.6 us (13%)
  blocking collectives  17.8 us (12%)
  between operations  13.3 us (9%)
  starting transfers between devices  13.1 us (9%)
  other arithmetic  10.2 us (7%)
  matrix products  6.73 us (5%)
    psum x2, waiting for transfers between devices, try_all_quarters(): return lax.psum(lax.psum(array_in, row_axis), mesh_ax)  43.3 us
    reduce_scatter x1, waiting for transfers between devices, per_device(): lax.psum_scatter(partial_grad, 'track', scatter_dimension=0, tiled=True)  19.6 us
    all_gather x1, blocking collectives, per_device(): every_block = lax.all_gather(rounded, 'track', axis=0, tiled=True)  14.5 us
    all_to_all x1, starting transfers between devices, per_device(): lax.all_to_all(labels, ('track', 'tm'), split_axis=0, concat_axis=0, tile...  7.25 us
    all_to_all x1, starting transfers between devices, per_device(): lax.all_to_all(outgoing, ('track', 'tm'), split_axis=0, concat_axis=0, ti...  5.72 us
    scatter x1, local copies, waits for them, and re-layouts, per_device(): jnp.zeros((6, sector_total * slot_count + 1), jnp.float32).at[:, target]  4.45 us
    scatter x1, local copies, waits for them, and re-layouts, per_device(): jnp.zeros((6, owners * capacity), jnp.float32).at[:, placing].set(payload)  4.36 us
    another operation x4, other arithmetic  4.31 us
  transfers between devices with their start and end apart: 5, of which 4 were waited for; matrix products, arithmetic and copies ran while one was open for 12% of the time, Pallas kernels for 0%

profile of v1, /device:TPU:0, one launch (start us, length us, event | category | flops | bytes accessed | tf_op | source)
XLA Modules:
  0.0 146.1 jit_solution(9573276944461057414)
XLA Ops:
  6.5 0.7 add_select_fusion
  7.2 1.7 %reduce-window.14 = s32[8,6,128]{2,0,1:T(8,128)S(1)} reduce-window(s32[8,6,128]{2,0,1:T(8,128)S(1)} %fusion.13, s32[]{:T(128)} %constant.40.clone.1), window={size=1x1x128 pad=0_0x0_0x127_0}, to_apply=%region_0.1 | reduce-window | flops 780288 | bytes 49156 | tf_op jit(solution)/shard_map/reduce-window
  8.9 0.1 slice.30
  9.0 0.1 copy.24
  9.2 0.2 reduce-window.15
  9.3 0.1 copy.25
  9.4 0.1 fusion.11
  9.5 3.4 %scatter_custom_fusion = s32[1536]{0:T(1024)S(1)} fusion(s32[768]{0:T(1024)S(1)} %compare_select_fusion.2, s32[768]{0:T(1024)S(1)} %get-tuple-element.7, s32[]{:T(128)} %constant.74.clone.1), kind=kCustom, calls=%fused_computation.50 | custom fusion | bytes 6148 | tf_op jit(solution)/shard_map/scatter | solution.py:27
  12.9 0.7 all_to_all.9
  13.6 7.3 %all-to-all-start = ((s32[8,1,192]{2,1,0:T(1,128)}), s32[8,1,192]{2,1,0:T(1,128)S(1)}, u32[]{:S(2)}, u32[]{:S(2)}) async-start(s32[8,1,192]{2,1,0:T(1,128)} %all_to_all.9), calls=%async_computation | async-start | bytes 16384 | tf_op jit(solution)/shard_map/all_to_all | solution.py:31
  20.8 0.7 compare_select_fusion.1
  21.5 0.8 reshape.166
  22.3 0.7 maximum_bitcast_fusion
  23.0 0.2 copy.26
  23.2 4.4 %scatter_custom_fusion.1 = f32[6,1536]{0,1:T(8,128)S(1)} fusion(s32[768]{0:T(1024)S(1)} %compare_select_fusion.2, f32[768,6]{1,0:T(8,128)S(1)} %copy.26, f32[]{:T(128)} %constant.39.clone.1), kind=kCustom, calls=%fused_computation.7 | custom fusion | bytes 36868 | tf_op jit(solution)/shard_map/scatter | solution.py:25
  27.6 1.0 copy.27
  28.6 0.9 convert_element_type.18
  29.5 14.5 %all_gather.3 = bf16[1024,128]{1,0:T(8,128)(2,1)S(1)} all-gather(bf16[256,128]{1,0:T(8,128)(2,1)S(1)} %convert_element_type.18), channel_id=1, replica_groups=mesh['parts'=2,'track'=4,'tm'=2,'coef'=2] {'track'}, dimensions={0}, use_global_device_ids=true | all-gather | bytes 327680 | tf_op jit(solution)/shard_map/all_gather | solution.py:18
  44.0 0.1 reshape.175
  44.0 0.6 gather_fusion
  44.7 0.8 compare_and_fusion
  45.4 0.1 select_bitcast_fusion
  45.5 3.7 %fusion = f32[8,1,3,128,1]{3,1,4,2,0:T(1,128)S(1)} fusion(bf16[8,6,3,128,128]{4,3,2,1,0:T(8,128)(2,1)} %param.13, bf16[8,6,128,1,1]{2,1,0,3,4:T(8,128)(2,1)S(1)} %select_bitcast_fusion), kind=kOutput, calls=%fused_computation.5 | convolution fusion | flops 4718592 | bytes 4743168 | tf_op jit(solution)/shard_map/skcjb,skb->scj/dot_general | solution.py:50
  49.2 3.3 %psum.21 = f32[8,3,128]{2,0,1:T(8,128)S(1)} all-reduce(f32[8,3,128]{2,0,1:T(8,128)S(1)} %bitcast.50), channel_id=1, replica_groups=mesh['parts'=2,'track'=4,'tm'=2,'coef'=2] {'coef'}, use_global_device_ids=true, to_apply=%region_9.10 | all-reduce | flops 3072 | bytes 24576 | tf_op jit(solution)/shard_map/psum | solution.py:53
  52.5 5.7 %all-to-all-start.1 = ((f32[8,6,192]{2,1,0:T(8,128)}), f32[8,6,192]{2,1,0:T(8,128)S(1)}, u32[]{:S(2)}, u32[]{:S(2)}) async-start(f32[8,6,192]{2,1,0:T(8,128)} %bitcast.8), calls=%async_computation.1 | async-start | bytes 131072 | tf_op jit(solution)/shard_map/all_to_all | solution.py:30
  58.2 0.0 reduce-scatter.2.cloned.1.call-start
  58.3 0.1 eq.61
  58.4 0.1 eq.57
  58.5 2.3 %reduce-window.16 = s32[8,12,128]{2,1,0:T(8,128)S(1)} reduce-window(s32[8,12,128]{2,1,0:T(8,128)S(1)} %fusion.8, s32[]{:T(128)} %constant.40.clone.1), window={size=1x1x128 pad=0_0x0_0x127_0}, to_apply=%region_4.5 | reduce-window | flops 1560576 | bytes 98308 | tf_op jit(solution)/shard_map/reduce-window.2
  60.7 0.3 slice_reduce_fusion
  61.0 0.2 reduce-window.19
  61.2 0.1 add_bitcast_fusion
  61.3 0.1 mul.43
  61.4 0.1 ge.21
  61.6 3.5 %all-to-all-done.1 = f32[8,6,192]{2,1,0:T(8,128)S(1)} async-done(((f32[8,6,192]{2,1,0:T(8,128)}), f32[8,6,192]{2,1,0:T(8,128)S(1)}, u32[]{:S(2)}, u32[]{:S(2)}) %all-to-all-start.1) | async-done | bytes 36896 | tf_op jit(solution)/shard_map/all_to_all | solution.py:30
  65.1 0.1 reshape.198
  65.2 0.3 copy.29
  65.5 4.4 %scatter_custom_fusion.2 = f32[6,1025]{0,1:T(8,128)S(1)} fusion(s32[1536]{0:T(1024)S(1)} %fusion.17, f32[1536,6]{1,0:T(8,128)S(1)} %copy.29, f32[]{:T(128)} %constant.39.clone.1), kind=kCustom, calls=%fused_computation.9 | custom fusion | bytes 24604 | tf_op jit(solution)/shard_map/scatter | solution.py:42
  70.0 0.2 copy.36
  70.2 3.1 %fusion.15 = f32[8,1,6,128,1]{3,1,4,2,0:T(1,128)S(1)} fusion(bf16[8,6,3,128,128]{4,3,2,1,0:T(8,128)(2,1)} %param.13, bf16[8,3,128,1,1]{2,0,1,3,4:T(8,128)(2,1)S(1)} %fusion.18), kind=kOutput, calls=%fused_computation.34 | convolution fusion | flops 4718592 | bytes 4749312 | tf_op jit(solution)/shard_map/skcjb,scj->skb/dot_general | solution.py:56
  73.3 0.1 bitcast_select_fusion
  73.4 1.5 %scatter_custom_fusion.3 = f32[1024,128]{1,0:T(8,128)} fusion(s32[48]{0:T(128)S(1)} %fusion.23, f32[48,128]{1,0:T(8,128)S(1)} %reshape.209, f32[]{:T(128)} %constant.39.clone.1), kind=kCustom, calls=%fused_computation.11 | custom fusion | flops 6144 | bytes 524292 | tf_op jit(solution)/shard_map/scatter-add | solution.py:60
  75.0 0.0 all-reduce.3.cloned.1.call-start
  75.0 19.6 %reduce-scatter.2.cloned.1.call-done = f32[256,128]{1,0:T(8,128)} async-done(((f32[1024,128]{1,0:T(8,128)}), f32[256,128]{1,0:T(8,128)}) %reduce-scatter.2.cloned.1.call-update) | async-done | bytes 131088 | tf_op jit(solution)/shard_map/reduce_scatter | solution.py:61
  94.7 0.0 all-reduce.5.cloned.1.call-start
  94.7 18.4 %all-reduce.3.cloned.1.call-done = f32[256,128]{1,0:T(8,128)} async-done(((f32[256,128]{1,0:T(8,128)}), f32[256,128]{1,0:T(8,128)}) %all-reduce.3.cloned.1.call-update) | async-done | bytes 131088 | tf_op jit(solution)/shard_map/psum | solution.py:64
  113.1 24.9 %all-reduce.5.cloned.1.call-done = f32[256,128]{1,0:T(8,128)} async-done(((f32[256,128]{1,0:T(8,128)}), f32[256,128]{1,0:T(8,128)}) %all-reduce.5.cloned.1.call-update) | async-done | bytes 131088 | tf_op jit(solution)/shard_map/psum | solution.py:64
  138.0 1.6 %copy.50 = f32[256,128]{1,0:T(8,128)} copy(f32[256,128]{1,0:T(8,128)} %all-reduce.5.cloned.1.call-done) | data formatting | bytes 262144
  (20 shorter events, 0.3 us)
Async XLA Ops:
  13.6 38.9 %all-to-all-start = ((s32[8,1,192]{2,1,0:T(1,128)}), s32[8,1,192]{2,1,0:T(1,128)S(1)}, u32[]{:S(2)}, u32[]{:S(2)}) async-start(s32[8,1,192]{2,1,0:T(1,128)} %all_to_all.9), calls=%async_computation | async-start | bytes 16384 | tf_op jit(solution)/shard_map/all_to_all | solution.py:31
  52.5 12.6 %all-to-all-start.1 = ((f32[8,6,192]{2,1,0:T(8,128)}), f32[8,6,192]{2,1,0:T(8,128)S(1)}, u32[]{:S(2)}, u32[]{:S(2)}) async-start(f32[8,6,192]{2,1,0:T(8,128)} %bitcast.8), calls=%async_computation.1 | async-start | bytes 131072 | tf_op jit(solution)/shard_map/all_to_all | solution.py:30
  58.2 36.4 %reduce-scatter.2.cloned.1.call-start = ((), (), s32[]{:S(2)}) async-start(), calls=%async_computation.3 | async-start | bytes 655360 | tf_op jit(solution)/shard_map/reduce_scatter | solution.py:61
  75.0 38.2 %all-reduce.3.cloned.1.call-start = ((), (), s32[]{:S(2)}) async-start(), calls=%async_computation.4 | async-start | bytes 262144 | tf_op jit(solution)/shard_map/psum | solution.py:64
  94.7 43.3 %all-reduce.5.cloned.1.call-start = ((), (), s32[]{:S(2)}) async-start(), calls=%async_computation.5 | async-start | bytes 262144 | tf_op jit(solution)/shard_map/psum | solution.py:64
Sparse Core Ops, SparseCore 0:
  75.1 19.5 reduce-scatter.1
  96.9 16.1 all-reduce.2
  115.4 22.5 all-reduce.4
